TPU v7x, 128 devices: a whole 4x4x4 slice. The times are simulated.
128 devices in a mesh: fsdp: 4 (over y_lo, core), dp: 32 (over z, x, y_hi).
Axes of the slice: x: 4, y: 4 (y_hi: 2, y_lo: 2; y = y_hi * 2 + y_lo), z: 4, core: 2. Of those that a mesh axis runs over, the one named last changes fastest.
Arguments:
- tokens: bfloat16 [65536, 1024], P(('fsdp', 'dp')), may hold values from -6 to 6
- norm_gain: bfloat16 [1024], P('fsdp'), may hold values from 0.25 to 1.75
- in_proj: bfloat16 [1024, 4384], P('fsdp'), may hold values from -0.1875 to 0.1875
- conv_weight: bfloat16 [4, 2304], P(None, 'fsdp'), may hold values from -0.796875 to 0.796875
- conv_bias: bfloat16 [2304], P('fsdp'), may hold values from -0.5 to 0.5
- dt_bias: bfloat16 [32], P('fsdp'), may hold values from -6 to -1
- a_log: bfloat16 [32], P('fsdp'), may hold values from 0 to 2.6875
- d_skip: bfloat16 [32], P('fsdp'), may hold values from 0.29882812 to 1.5
- gate_gain: bfloat16 [2048], P('fsdp'), may hold values from 0.25 to 1.75
- out_proj: bfloat16 [2048, 1024], P('fsdp'), may hold values from -0.125 to 0.125
- out_grad: bfloat16 [65536, 1024], P(('fsdp', 'dp')), may hold values from -6 to 6
- lengths: int32 [256], P(('fsdp', 'dp')), may hold values from 1 to 256, as said below
Outputs:
- block_out: bfloat16 [65536, 1024], P(('fsdp', 'dp'))
- tokens_grad: float32 [65536, 1024], P(('fsdp', 'dp'))
- norm_gain_grad: float32 [1024], P('fsdp')
- in_proj_grad: float32 [1024, 4384], P('fsdp')
- conv_weight_grad: float32 [4, 2304], P(None, 'fsdp')
- conv_bias_grad: float32 [2304], P('fsdp')
- dt_bias_grad: float32 [32], P('fsdp')
- a_log_grad: float32 [32], P('fsdp')
- d_skip_grad: float32 [32], P('fsdp')
- gate_gain_grad: float32 [2048], P('fsdp')
- out_proj_grad: float32 [2048, 1024], P('fsdp')
Inputs may be any that keep to these rules, and one draw needn't show every extreme that they name: `lengths`: every slot holds between one and 256 live rows; some slot is full in every draw.
All inputs are finite; a program needn't handle non-finite values.
Results may differ from a plain program's by a relative error of at most 0.025.
Values may be sent and summed in bfloat16 or wider, within the bound.
No kernel may reach another device: no remote copies, remote signals or barrier semaphores. Data moves between devices by JAX's collectives and lax.ppermute only.
A program may use at most 192 MiB of HBM per device.

v0:
```python
import jax
import jax.numpy as jnp
from jax import lax
from jax.sharding import PartitionSpec as P

LEN = 256


def make_rounders():

    def round_value(v):
        return lax.optimization_barrier(v.astype(jnp.bfloat16)).astype(jnp.float32)

    def plain_value(v):
        return v

    round_low = jax.custom_vjp(round_value)
    round_back = jax.custom_vjp(plain_value)

    def keep_low(v):
        return (round_value(v), None)

    def pass_low(kept, grad):
        return (grad,)

    def keep_back(v):
        return (v, None)

    def pass_back(kept, grad):
        return (round_value(grad),)

    round_low.defvjp(keep_low, pass_low)
    round_back.defvjp(keep_back, pass_back)
    return (round_low, round_back)


def slot_out(rounders, params, inputs, count):
    round_low, round_back = rounders
    norm_gain, in_proj, conv_weight, conv_bias, dt_bias, a_log, d_skip, gate_gain, out_proj = params
    rows = inputs.shape[0]
    inner = out_proj.shape[0]
    heads = a_log.shape[0]
    channels = conv_weight.shape[1]
    state = (channels - inner) // 2
    taps = conv_weight.shape[0]
    normed_in = round_low(
        inputs * lax.rsqrt(jnp.mean(inputs * inputs, axis=1, keepdims=True) + 1e-05) * norm_gain
    )
    proj = round_back(jnp.dot(normed_in, in_proj, preferred_element_type=jnp.float32))
    gate_part = proj[:, :inner]
    conv_in = proj[:, inner : inner + channels]
    step_raw = proj[:, inner + channels :]
    padded = jnp.concatenate([jnp.zeros((taps - 1, channels), jnp.float32), conv_in], axis=0)
    conv_sum = conv_bias[None, :] + padded[0:rows] * conv_weight[0][None, :]
    for index in range(1, taps):
        conv_sum = conv_sum + padded[index : index + rows] * conv_weight[index][None, :]
    conv_act = jax.nn.silu(conv_sum)
    values = round_low(conv_act[:, :inner])
    bmat = round_low(conv_act[:, inner : inner + state])
    cmat = round_low(conv_act[:, inner + state :])
    step = jax.nn.softplus(step_raw + dt_bias[None, :])
    logdecay = -step * jnp.exp(a_log)[None, :]
    cum = jnp.cumsum(logdecay, axis=0).T
    causal = (jnp.arange(rows)[:, None] >= jnp.arange(rows)[None, :])[None, :, :]
    spread = jnp.where(causal, cum[:, :, None] - cum[:, None, :], 0.0)
    decay = jnp.where(causal, jnp.exp(spread), 0.0)
    scores = round_back(jnp.dot(cmat, bmat.T, preferred_element_type=jnp.float32))
    mix = round_low(scores[None, :, :] * decay * step.T[:, None, :])
    heads_in = values.reshape(rows, heads, inner // heads)
    summed = round_back(
        jnp.einsum("hij,jhp->ihp", mix, heads_in, preferred_element_type=jnp.float32)
    )
    scanned = (summed + d_skip[None, :, None] * heads_in).reshape(rows, inner)
    gated = scanned * jax.nn.silu(gate_part)
    mixed_in = round_low(
        gated * lax.rsqrt(jnp.mean(gated * gated, axis=1, keepdims=True) + 1e-05) * gate_gain
    )
    result = inputs + jnp.dot(mixed_in, out_proj, preferred_element_type=jnp.float32)
    live = jnp.arange(rows) < count
    return jnp.where(live[:, None], result, 0.0)


def local(
    tokens,
    norm_gain,
    in_proj,
    conv_weight,
    conv_bias,
    dt_bias,
    a_log,
    d_skip,
    gate_gain,
    out_proj,
    out_grad,
    lengths,
):
    rounders = make_rounders()
    whole = (
        lax.all_gather(norm_gain, "fsdp", axis=0, tiled=True),
        lax.all_gather(in_proj, "fsdp", axis=0, tiled=True),
        lax.all_gather(conv_weight, "fsdp", axis=1, tiled=True),
        lax.all_gather(conv_bias, "fsdp", axis=0, tiled=True),
        lax.all_gather(dt_bias, "fsdp", axis=0, tiled=True),
        lax.all_gather(a_log, "fsdp", axis=0, tiled=True),
        lax.all_gather(d_skip, "fsdp", axis=0, tiled=True),
        lax.all_gather(gate_gain, "fsdp", axis=0, tiled=True),
        lax.all_gather(out_proj, "fsdp", axis=0, tiled=True),
    )
    params = tuple((weight.astype(jnp.float32) for weight in whole))
    inputs = tokens.astype(jnp.float32)
    slots = lengths.shape[0]
    width = inputs.shape[1]

    def forward(weights, rows_in):
        blocks = rows_in.reshape(slots, LEN, width)
        result = lax.map(
            jax.checkpoint(lambda item: slot_out(rounders, weights, item[0], item[1])),
            (blocks, lengths),
        )
        return result.reshape(slots * LEN, width)

    result, pullback = jax.vjp(forward, params, inputs)
    grads, tokens_grad = pullback(out_grad.astype(jnp.float32))
    g_norm, g_inproj, g_convw, g_convb, g_dtbias, g_alog, g_skip, g_gate, g_outproj = grads
    owned = (
        lax.psum_scatter(
            g_norm.astype(jnp.bfloat16), "fsdp", scatter_dimension=0, tiled=True
        ).astype(jnp.float32),
        lax.psum_scatter(
            g_inproj.astype(jnp.bfloat16), "fsdp", scatter_dimension=0, tiled=True
        ).astype(jnp.float32),
        lax.psum_scatter(
            g_convw.astype(jnp.bfloat16), "fsdp", scatter_dimension=1, tiled=True
        ).astype(jnp.float32),
        lax.psum_scatter(
            g_convb.astype(jnp.bfloat16), "fsdp", scatter_dimension=0, tiled=True
        ).astype(jnp.float32),
        lax.psum_scatter(
            g_dtbias.astype(jnp.bfloat16), "fsdp", scatter_dimension=0, tiled=True
        ).astype(jnp.float32),
        lax.psum_scatter(
            g_alog.astype(jnp.bfloat16), "fsdp", scatter_dimension=0, tiled=True
        ).astype(jnp.float32),
        lax.psum_scatter(
            g_skip.astype(jnp.bfloat16), "fsdp", scatter_dimension=0, tiled=True
        ).astype(jnp.float32),
        lax.psum_scatter(
            g_gate.astype(jnp.bfloat16), "fsdp", scatter_dimension=0, tiled=True
        ).astype(jnp.float32),
        lax.psum_scatter(
            g_outproj.astype(jnp.bfloat16), "fsdp", scatter_dimension=0, tiled=True
        ).astype(jnp.float32),
    )
    s_norm, s_inproj, s_convw, s_convb, s_dtbias, s_alog, s_skip, s_gate, s_outproj = owned
    final = (
        lax.psum(s_norm.astype(jnp.bfloat16), "dp").astype(jnp.float32),
        lax.psum(s_inproj.astype(jnp.bfloat16), "dp").astype(jnp.float32),
        lax.psum(s_convw.astype(jnp.bfloat16), "dp").astype(jnp.float32),
        lax.psum(s_convb.astype(jnp.bfloat16), "dp").astype(jnp.float32),
        lax.psum(s_dtbias.astype(jnp.bfloat16), "dp").astype(jnp.float32),
        lax.psum(s_alog.astype(jnp.bfloat16), "dp").astype(jnp.float32),
        lax.psum(s_skip.astype(jnp.bfloat16), "dp").astype(jnp.float32),
        lax.psum(s_gate.astype(jnp.bfloat16), "dp").astype(jnp.float32),
        lax.psum(s_outproj.astype(jnp.bfloat16), "dp").astype(jnp.float32),
    )
    return (
        result.astype(jnp.bfloat16),
        tokens_grad,
        final[0],
        final[1],
        final[2],
        final[3],
        final[4],
        final[5],
        final[6],
        final[7],
        final[8],
    )


def solution(mesh):
    in_specs = (
        P(("fsdp", "dp"), None),
        P("fsdp"),
        P("fsdp", None),
        P(None, "fsdp"),
        P("fsdp"),
        P("fsdp"),
        P("fsdp"),
        P("fsdp"),
        P("fsdp"),
        P("fsdp", None),
        P(("fsdp", "dp"), None),
        P(("fsdp", "dp")),
    )
    out_specs = (
        P(("fsdp", "dp"), None),
        P(("fsdp", "dp"), None),
        P("fsdp"),
        P("fsdp", None),
        P(None, "fsdp"),
        P("fsdp"),
        P("fsdp"),
        P("fsdp"),
        P("fsdp"),
        P("fsdp"),
        P("fsdp", None),
    )
    return jax.shard_map(local, mesh=mesh, in_specs=in_specs, out_specs=out_specs, check_vma=False)
```

profile of v0, /device:TPU:8, one launch (start us, length us, event | category | flops | bytes accessed | tf_op | source)
XLA Modules:
  0.0 925.3 jit_solution(12131785813211535580)
XLA Ops:
  15.4 5.8 all-reduce.29
  42.3 14.7 %all-gather.8.cloned.1.call-done = bf16[2048,1024]{1,0:T(8,128)(2,1)} async-done(((bf16[512,1024]{1,0:T(8,128)(2,1)}), bf16[2048,1024]{1,0:T(8,128)(2,1)}) %all-gather.8.cloned.1.call-update) | async-done | bytes 4194320 | tf_op jit(solution)/shard_map/all_gather | solution.py:107
  57.0 91.1 %all-gather.6.cloned.1.call-done = bf16[1024,4384]{1,0:T(8,128)(2,1)} async-done(((bf16[256,4384]{1,0:T(8,128)(2,1)}), bf16[1024,4384]{1,0:T(8,128)(2,1)}) %all-gather.6.cloned.1.call-update) | async-done | bytes 8978448 | tf_op jit(solution)/shard_map/all_gather | solution.py:100
  149.6 232.5 %while.48 = (s32[]{:T(128)}, f32[1024]{0:T(1024)}, f32[1024,4384]{0,1:T(8,128)}, f32[2304]{0:T(1024)}, f32[4,2304]{1,0:T(4,128)}, /*index=5*/f32[32]{0:T(128)}, ...) while((s32[]{:T(128)}, f32[1024]{0:T(1024)}, ...), condition=%wide.region_30.31_spmd.clone, body=%wide.region_6.30_spmd.clone.sunk | while | flops 10011840512 | bytes 402432256 | solution.py:116
  172.1 7.7 fusion.180
  180.2 5.5 multiply_convert_fusion.17
  212.4 7.0 fusion.184
  235.2 5.6 multiply_reduce_fusion.26
  250.3 9.8 %select_add_fusion.13 = f32[1024,4384]{0,1:T(8,128)} fusion(f32[1024,4384]{0,1:T(8,128)} %get-tuple-element.1465, bf16[256,4384]{0,1:T(8,128)(2,1)S(1)} %add_convert_fusion.2, bf16[256,1024]{1,0:T(8,128)(2,1)} %copy-done.17, pred[]{:T(512)S(6)} %compare.19), kind=kOutput, calls=%fused_computation.38.clone.1 | convolution fusion | flops 2307457024 | bytes 38682624 | tf_op jit(solution)/shard_map/transpose(jvp())/while/body/eval_jaxpr/checkpoint/dot_general | solution.py:49
  270.7 7.7 fusion.180
  311.0 7.0 fusion.184
  333.8 5.6 multiply_reduce_fusion.26
  348.9 15.1 %select_add_fusion.13 = f32[1024,4384]{0,1:T(8,128)} fusion(f32[1024,4384]{0,1:T(8,128)} %get-tuple-element.1465, bf16[256,4384]{0,1:T(8,128)(2,1)S(1)} %add_convert_fusion.2, bf16[256,1024]{1,0:T(8,128)(2,1)} %copy-done.17, pred[]{:T(512)S(6)} %compare.19), kind=kOutput, calls=%fused_computation.38.clone.1 | convolution fusion | flops 2307457024 | bytes 38682624 | tf_op jit(solution)/shard_map/transpose(jvp())/while/body/eval_jaxpr/checkpoint/dot_general | solution.py:49
  364.2 8.2 select_add_fusion.17
  382.1 6.1 convert_element_type.270
  388.3 9.5 %convert_element_type.256 = bf16[1024,4384]{0,1:T(8,128)(2,1)} convert(f32[1024,4384]{0,1:T(8,128)} %get-tuple-element.689) | non-fusion elementwise | flops 4489216 | bytes 26935296 | tf_op jit(solution)/shard_map/convert_element_type | solution.py:130
  404.2 30.7 %reduce-scatter.8.cloned.1.call-done = bf16[512,1024]{1,0:T(8,128)(2,1)} async-done(((bf16[2048,1024]{1,0:T(8,128)(2,1)}), bf16[512,1024]{1,0:T(8,128)(2,1)}) %reduce-scatter.8.cloned.1.call-update) | async-done | bytes 1048592 | tf_op jit(solution)/shard_map/reduce_scatter | solution.py:150
  435.0 87.3 %reduce-scatter.6.cloned.1.call-done = bf16[256,4384]{0,1:T(8,128)(2,1)} async-done(((bf16[1024,4384]{0,1:T(8,128)(2,1)}), bf16[256,4384]{0,1:T(8,128)(2,1)}) %reduce-scatter.6.cloned.1.call-update) | async-done | bytes 2244624 | tf_op jit(solution)/shard_map/reduce_scatter | solution.py:129
  522.3 66.8 %while.47 = (s32[]{:T(128)}, bf16[2,256,1024]{2,1,0:T(8,128)(2,1)}, s32[2]{0:T(128)}, f32[2,256,1024]{2,1,0:T(8,128)S(1)}, f32[1,2304]{1,0:T(1,128)}, /*index=5*...) while((s32[]{:T(128)}, bf16[2,256,1024]{2,1,0:T(8,128)(2,1)}, ...), condition=%wide.region_5.6_spmd.clone.clone, body=%wide.region_0.5_spmd.clone.clone.sunk | while | flops 3687457536 | bytes 117013696 | solution.py:116
  523.6 7.5 fusion.155
  557.0 7.5 fusion.155
  593.0 12.5 %all-reduce.28 = (bf16[1024]{0:T(1024)(128)(2,1)S(1)}, bf16[2304]{0:T(1024)(128)(2,1)S(1)}, bf16[32]{0:T(256)(128)(2,1)S(1)}, bf16[32]{0:T(256)(128)(2,1)S(1)}, ...) all-reduce(bf16[1024]{0:T(1024)(128)(2,1)S(1)} %convert_element_typ, ...), channel_id=2, replica_groups=mesh['fsdp'=4,'dp'=32] {'fsdp'}, use_global_device_ids=true, to_apply=%region_31.32.clone | all-reduce | flops 5472 | bytes 21888
  607.0 182.9 %all-reduce.26 = (bf16[256]{0:T(256)(128)(2,1)S(1)}, bf16[4,576]{1,0:T(4,128)(2,1)S(1)}, bf16[576]{0:T(1024)(128)(2,1)S(1)}, bf16[8]{0:T(256)(128)(2,1)S(1)}, bf...) all-reduce(bf16[256]{0:T(256)(128)(2,1)S(1)} %dynamic-slice.5, ...), channel_id=1, replica_groups=mesh['fsdp'=4,'dp'=32] {'dp'}, use_global_device_ids=true, to_apply=%region_32.33 | all-reduce | flops 3672 | bytes 14688 | tf_op jit(solution)/shard_map/psum | solution.py:156
  793.8 118.7 %all-reduce.32.cloned.1.call-done = (bf16[256,4384]{0,1:T(8,128)(2,1)}, bf16[512,1024]{1,0:T(8,128)(2,1)}) async-done(((bf16[256,4384]{0,1:T(8,128)(2,1)}, bf16[512,1024]{1,0:T(8,128)(2,1)}), (bf16[256,4384]{0,1:T(8,128)(2,1)}, bf16[512,1024]{1,0:T(8,128)(2,1)})) %all-reduce.32.cloned.1.call-update) | async-done | bytes 3293200 | tf_op jit(solution)/shard_map/psum | solution.py:157
  (590 shorter events, 224.7 us)
Async XLA Ops:
  7.2 49.8 %all-gather.8.cloned.1.call-start = ((), (), s32[]{:S(2)}) async-start(), calls=%async_computation.4 | async-start | bytes 5242880 | tf_op jit(solution)/shard_map/all_gather | solution.py:107
  8.0 14.4 %copy-start.34 = (bf16[512,1024]{1,0:T(8,128)(2,1)S(1)}, bf16[512,1024]{1,0:T(8,128)(2,1)}, u32[]{:S(2)}) copy-start(bf16[512,1024]{1,0:T(8,128)(2,1)} %param.16) | copy-start | bytes 3145732
  8.0 140.1 %all-gather.6.cloned.1.call-start = ((), (), s32[]{:S(2)}) async-start(), calls=%async_computation.3 | async-start | bytes 11468800 | tf_op jit(solution)/shard_map/all_gather | solution.py:100
  12.3 15.8 %copy-start.81 = (bf16[512]{0:T(512)(128)(2,1)S(1)}, bf16[512]{0:T(512)(128)(2,1)}, u32[]{:S(2)}) copy-start(bf16[512]{0:T(512)(128)(2,1)} %param.24) | copy-start | bytes 3076
  12.3 21.6 %copy-start.87 = (bf16[256]{0:T(256)(128)(2,1)S(1)}, bf16[256]{0:T(256)(128)(2,1)}, u32[]{:S(2)}) copy-start(bf16[256]{0:T(256)(128)(2,1)} %param.17) | copy-start | bytes 1540
  12.3 422.7 %reduce-scatter.8.cloned.1.call-start = ((), (), s32[]{:S(2)}) async-start(), calls=%async_computation.6 | async-start | bytes 5242880 | tf_op jit(solution)/shard_map/reduce_scatter | solution.py:150
  21.2 20.5 %copy-start.88 = (bf16[32]{0:T(256)(128)(2,1)}, bf16[32]{0:T(256)(128)(2,1)S(1)}, u32[]{:S(2)}) copy-start(bf16[32]{0:T(256)(128)(2,1)S(1)} %get-tuple-element.973) | copy-start | bytes 196
  167.4 12.7 %copy-start.29 = (f32[4,2304]{1,0:T(4,128)}, f32[4,2304]{1,0:T(4,128)S(1)}, u32[]{:S(2)}) copy-start(f32[4,2304]{1,0:T(4,128)S(1)} %get-tuple-element.1329) | copy-start | bytes 110596 | tf_op jit(solution)/shard_map/transpose(jvp())/while
  266.0 12.7 %copy-start.29 = (f32[4,2304]{1,0:T(4,128)}, f32[4,2304]{1,0:T(4,128)S(1)}, u32[]{:S(2)}) copy-start(f32[4,2304]{1,0:T(4,128)S(1)} %get-tuple-element.1329) | copy-start | bytes 110596 | tf_op jit(solution)/shard_map/transpose(jvp())/while
  348.8 15.2 %copy-start.32 = (f32[4,2304]{1,0:T(4,128)}, f32[4,2304]{1,0:T(4,128)S(1)}, u32[]{:S(2)}) copy-start(f32[4,2304]{1,0:T(4,128)S(1)} %select_add_fusion.15) | copy-start | bytes 110596 | tf_op jit(solution)/shard_map/transpose(jvp())/while
  348.9 15.2 %copy-start.58 = (f32[1024]{0:T(1024)S(1)}, f32[1024]{0:T(1024)}, u32[]{:S(2)}) copy-start(f32[1024]{0:T(1024)} %get-tuple-element.1464) | copy-start | bytes 12292 | tf_op jit(solution)/shard_map/transpose(jvp())/while
  348.9 15.2 %copy-start.65 = (f32[32]{0:T(128)S(1)}, f32[32]{0:T(128)}, u32[]{:S(2)}) copy-start(f32[32]{0:T(128)} %get-tuple-element.1371) | copy-start | bytes 388 | tf_op jit(solution)/shard_map/transpose(jvp())/while
  348.9 15.2 %copy-start.71 = (f32[32]{0:T(128)S(1)}, f32[32]{0:T(128)}, u32[]{:S(2)}) copy-start(f32[32]{0:T(128)} %get-tuple-element.1336) | copy-start | bytes 388 | tf_op jit(solution)/shard_map/transpose(jvp())/while
  348.9 15.2 %copy-start.72 = (f32[32]{0:T(128)S(1)}, f32[32]{0:T(128)}, u32[]{:S(2)}) copy-start(f32[32]{0:T(128)} %get-tuple-element.1469) | copy-start | bytes 388 | tf_op jit(solution)/shard_map/transpose(jvp())/while
  348.9 15.2 %copy-start.66 = (f32[32]{0:T(128)S(1)}, f32[32]{0:T(128)}, u32[]{:S(2)}) copy-start(f32[32]{0:T(128)} %get-tuple-element.1370) | copy-start | bytes 388 | tf_op jit(solution)/shard_map/transpose(jvp())/while
  348.9 15.2 %copy-start.74 = (f32[32]{0:T(128)S(1)}, f32[32]{0:T(128)}, u32[]{:S(2)}) copy-start(f32[32]{0:T(128)} %get-tuple-element.1468) | copy-start | bytes 388 | tf_op jit(solution)/shard_map/transpose(jvp())/while
  348.9 15.2 %copy-start.6 = (f32[256,1024]{1,0:T(8,128)S(1)}, f32[256,1024]{1,0:T(8,128)}, u32[]{:S(2)}) copy-start(f32[256,1024]{1,0:T(8,128)} %get-tuple-element.1347) | copy-start | bytes 3145732 | tf_op jit(solution)/shard_map/transpose(jvp())/while
  348.9 15.2 %copy-start.18 = (bf16[256,2048]{0,1:T(8,128)(2,1)S(1)}, bf16[256,2048]{0,1:T(8,128)(2,1)}, u32[]{:S(2)}) copy-start(bf16[256,2048]{0,1:T(8,128)(2,1)} %get-tuple-element.1374) | copy-start | bytes 3145732 | tf_op jit(solution)/shard_map/transpose(jvp())/while
  388.2 134.0 %reduce-scatter.6.cloned.1.call-start = ((), (), s32[]{:S(2)}) async-start(), calls=%async_computation.5 | async-start | bytes 11223040 | tf_op jit(solution)/shard_map/reduce_scatter | solution.py:129
  397.8 208.2 %reduce-scatter.10.cloned.1.call-start = ((), (), s32[]{:S(2)}) async-start(), calls=%async_computation.7 | async-start | bytes 737280
  400.7 511.8 %all-reduce.32.cloned.1.call-start = ((), (), s32[]{:S(2)}) async-start(), calls=%async_computation.8 | async-start | bytes 6586368 | tf_op jit(solution)/shard_map/psum | solution.py:157
  522.3 12.4 %copy-start.49 = (f32[1,2304]{1,0:T(1,128)}, f32[1,2304]{1,0:T(1,128)S(1)}, u32[]{:S(2)}) copy-start(f32[1,2304]{1,0:T(1,128)S(1)} %get-tuple-element.1424) | copy-start | bytes 27652 | tf_op jit(solution)/shard_map/jvp()/while
  555.7 11.8 %copy-start.47 = (f32[1,2304]{1,0:T(1,128)}, f32[1,2304]{1,0:T(1,128)S(1)}, u32[]{:S(2)}) copy-start(f32[1,2304]{1,0:T(1,128)S(1)} %get-tuple-element.1425) | copy-start | bytes 27652 | tf_op jit(solution)/shard_map/jvp()/while
  555.7 12.4 %copy-start.49 = (f32[1,2304]{1,0:T(1,128)}, f32[1,2304]{1,0:T(1,128)S(1)}, u32[]{:S(2)}) copy-start(f32[1,2304]{1,0:T(1,128)S(1)} %get-tuple-element.1424) | copy-start | bytes 27652 | tf_op jit(solution)/shard_map/jvp()/while
  (153 other events, 714.2 us)
Sparse Core Ops, SparseCore 0:
  9.7 47.2 all-gather.7
  59.2 88.8 all-gather.5
  388.4 46.5 reduce-scatter.7
  437.4 84.7 reduce-scatter.5
  524.6 19.3 reduce-scatter.9
  546.7 365.7 all-reduce.31
where the time goes:
time: 931 us; the launch traced here: 925 us
  waiting for transfers between devices  343 us (37%)
  blocking collectives  217 us (23%)
  other arithmetic  145 us (16%)
  matrix products  117 us (13%)
  local copies, waits for them, and re-layouts  55.7 us (6%)
  loops' own time  28.9 us (3%)
  between operations  18.1 us (2%)
    psum x1, blocking collectives, local(): lax.psum(s_norm.astype(jnp.bfloat16), 'dp').astype(jnp.float32)  183 us
    psum x1, waiting for transfers between devices, local(): lax.psum(s_inproj.astype(jnp.bfloat16), 'dp').astype(jnp.float32)  119 us
    all_gather x1, waiting for transfers between devices, local(): lax.all_gather(in_proj, 'fsdp', axis=0, tiled=True)  91.1 us
    reduce_scatter x1, waiting for transfers between devices, local(): lax.psum_scatter(g_inproj.astype(jnp.bfloat16), 'fsdp', scatter_dimension...  87.3 us
    dot_general x8, matrix products, slot_out(): jnp.dot(normed_in, in_proj, preferred_element_type=jnp.float32)  60.9 us
    another operation x20, other arithmetic  40.3 us
    reduce_scatter x1, waiting for transfers between devices, local(): lax.psum_scatter(g_outproj.astype(jnp.bfloat16), 'fsdp', scatter_dimensio...  30.7 us
    another operation x2, loops' own time, forward(): lax.map(jax.checkpoint(lambda item: slot_out(rounders, weights, item[0],...  28.9 us
  transfers between devices with their start and end apart: 6, of which 5 were waited for; matrix products, arithmetic and copies ran while one was open for 10% of the time, Pallas kernels for 0%

commit v1 on v0

v1 whole, which is shorter than its diff:
```python
import functools
import jax
import jax.numpy as jnp
from jax import lax
from jax.experimental import pallas as pl
from jax.experimental.pallas import tpu as pltpu
from jax.sharding import Mesh, PartitionSpec as P

D = 1024
INNER = 2048
CONV = 4
LEN = 256
HEADS = 32
STATE = 128
CONVCH = 2304
HALF = 128
GROUPS = 4
GCOLS = INNER // GROUPS
GHEADS = HEADS // GROUPS
BF = jnp.bfloat16
F32 = jnp.float32
LOG2E = 1.4426950408889634
VMEM_LIMIT = 50 * 1024 * 1024


def dot(a, b):
    return lax.dot_general(a, b, (((1,), (0,)), ((), ())), preferred_element_type=F32)


def dot_nt(a, b):
    return lax.dot_general(a, b, (((1,), (1,)), ((), ())), preferred_element_type=F32)


def dot_tn(a, b):
    return lax.dot_general(a, b, (((0,), (0,)), ((), ())), preferred_element_type=F32)


def dot_exact(ones, v):
    hi = v.astype(BF)
    rest = v - hi.astype(F32)
    mid = rest.astype(BF)
    low = (rest - mid.astype(F32)).astype(BF)
    return dot(ones, hi) + dot(ones, mid) + dot(ones, low)


def dot_split(v, ones):
    hi = v.astype(BF)
    low = (v - hi.astype(F32)).astype(BF)
    return dot(hi, ones) + dot(low, ones)


def sigmoid(v):
    return 0.5 * jnp.tanh(0.5 * v) + 0.5


def rows_down(v, count):
    row = lax.broadcasted_iota(jnp.int32, v.shape, 0)
    return jnp.where(row >= count, pltpu.roll(v, count, axis=0), 0.0)


def rows_up(v, count):
    rows = v.shape[0]
    row = lax.broadcasted_iota(jnp.int32, v.shape, 0)
    return jnp.where(row < rows - count, pltpu.roll(v, rows - count, axis=0), 0.0)


def conv_forward(x, taps, bias):
    total = bias + taps[3:4] * x
    for back in range(1, CONV):
        total = total + taps[3 - back : 4 - back] * rows_down(x, back)
    return total


def conv_backward(x, taps, bias, dact, dtaps_ref, columns):
    v = conv_forward(x, taps, bias)
    sg = sigmoid(v)
    dv = dact * (sg * (1.0 + v * (1.0 - sg)))
    dx = taps[3:4] * dv
    sums = [jnp.sum(dv * x, axis=0, keepdims=True)]
    for back in range(1, CONV):
        dx = dx + taps[3 - back : 4 - back] * rows_up(dv, back)
        sums.insert(0, jnp.sum(dv * rows_down(x, back), axis=0, keepdims=True))
    sums.append(jnp.sum(dv, axis=0, keepdims=True))
    sums.append(jnp.zeros((3, x.shape[1]), F32))
    dtaps_ref[0, :, columns] = jnp.concatenate(sums, axis=0)
    return dx


def step_of(raw, bias):
    z = raw + bias
    return jnp.maximum(z, 0.0) + jnp.log1p(jnp.exp(-jnp.abs(z)))


def tri_masks():
    down = lax.broadcasted_iota(jnp.int32, (HALF, HALF), 0)
    across = lax.broadcasted_iota(jnp.int32, (HALF, HALF), 1)
    return down, across


def head_lanes(v, first):
    lane = lax.broadcasted_iota(jnp.int32, v.shape, 1)
    zero = jnp.zeros_like(v)
    return jnp.where(lane < 64, v, zero) if first else jnp.where(lane < 64, zero, v)


def scan_forward_kernel(
    xv_ref, xbc_ref, raw_ref, tv_ref, tbc_ref, dtb_ref, alog_ref,
    summed_ref, v_ref, bc_ref, step_ref, cum_ref,
    s_ref, cumt_ref, stept_ref,
):
    group = pl.program_id(1)

    @pl.when(group == 0)
    def _():
        act = conv_forward(xbc_ref[...], tbc_ref[0:4, :], tbc_ref[4:5, :])
        bc = (act * sigmoid(act)).astype(BF)
        bc_ref[...] = bc
        s_ref[...] = dot_nt(bc[:, STATE:], bc[:, :STATE])
        step = step_of(raw_ref[...], dtb_ref[...])
        logdecay = -step * jnp.exp(alog_ref[...])
        row = lax.broadcasted_iota(jnp.int32, (LEN, LEN), 0)
        col = lax.broadcasted_iota(jnp.int32, (LEN, LEN), 1)
        lower = jnp.where(row >= col, 1.0, 0.0).astype(BF)
        cum = dot_exact(lower, logdecay) * LOG2E
        step_ref[...] = step
        cum_ref[...] = cum
        cumt_ref[...] = cum.T
        stept_ref[...] = step.T

    act = conv_forward(xv_ref[...], tv_ref[0:4, :], tv_ref[4:5, :])
    v_ref[...] = (act * sigmoid(act)).astype(BF)
    cols = pltpu.roll(cum_ref[...], lax.rem(128 - GHEADS * group, 128), axis=1)
    first = pl.multiple_of(GHEADS * group, GHEADS)
    cum_rows = cumt_ref[pl.ds(first, GHEADS), :]
    step_rows = stept_ref[pl.ds(first, GHEADS), :]
    down, across = tri_masks()
    live = down >= across
    for pair in range(GHEADS // 2):
        lanes = slice(128 * pair, 128 * pair + 128)
        vp = v_ref[:, lanes]
        top = jnp.zeros((HALF, 128), F32)
        bottom = jnp.zeros((HALF, 128), F32)
        for side in range(2):
            head = 2 * pair + side
            vm = head_lanes(vp, side == 0)
            ci = cols[:, head : head + 1]
            cj = cum_rows[head : head + 1, :]
            sj = step_rows[head : head + 1, :]
            w00 = jnp.where(live, jnp.exp2(ci[:HALF] - cj[:, :HALF]), 0.0) * sj[:, :HALF]
            w10 = jnp.exp2(ci[HALF:] - cj[:, :HALF]) * sj[:, :HALF]
            w11 = jnp.where(live, jnp.exp2(ci[HALF:] - cj[:, HALF:]), 0.0) * sj[:, HALF:]
            m00 = (s_ref[:HALF, :HALF] * w00).astype(BF)
            m10 = (s_ref[HALF:, :HALF] * w10).astype(BF)
            m11 = (s_ref[HALF:, HALF:] * w11).astype(BF)
            top = top + dot(m00, vm[:HALF])
            bottom = bottom + dot(jnp.concatenate([m10, m11], axis=1), vm)
        summed_ref[:HALF, lanes] = top
        summed_ref[HALF:, lanes] = bottom


def scan_forward(xconv, raw, taps, dtb, alog, slots):
    rows = slots * LEN
    by_slot = lambda slot, group: (slot, 0)
    fixed = lambda slot, group: (0, 0)
    return pl.pallas_call(
        scan_forward_kernel,
        grid=(slots, GROUPS),
        in_specs=[
            pl.BlockSpec((LEN, GCOLS), lambda slot, group: (slot, group)),
            pl.BlockSpec((LEN, 2 * STATE), lambda slot, group: (slot, INNER // (2 * STATE))),
            pl.BlockSpec((LEN, 128), by_slot),
            pl.BlockSpec((8, GCOLS), lambda slot, group: (0, group)),
            pl.BlockSpec((8, 2 * STATE), lambda slot, group: (0, INNER // (2 * STATE))),
            pl.BlockSpec((1, 128), fixed),
            pl.BlockSpec((1, 128), fixed),
        ],
        out_specs=[
            pl.BlockSpec((LEN, GCOLS), lambda slot, group: (slot, group)),
            pl.BlockSpec((LEN, GCOLS), lambda slot, group: (slot, group)),
            pl.BlockSpec((LEN, 2 * STATE), by_slot),
            pl.BlockSpec((LEN, 128), by_slot),
            pl.BlockSpec((LEN, 128), by_slot),
        ],
        out_shape=[
            jax.ShapeDtypeStruct((rows, INNER), F32),
            jax.ShapeDtypeStruct((rows, INNER), BF),
            jax.ShapeDtypeStruct((rows, 2 * STATE), BF),
            jax.ShapeDtypeStruct((rows, 128), F32),
            jax.ShapeDtypeStruct((rows, 128), F32),
        ],
        scratch_shapes=[
            pltpu.VMEM((LEN, LEN), F32),
            pltpu.VMEM((128, LEN), F32),
            pltpu.VMEM((128, LEN), F32),
        ],
        compiler_params=pltpu.CompilerParams(
            dimension_semantics=("arbitrary", "arbitrary"), vmem_limit_bytes=VMEM_LIMIT
        ),
        name="scan_forward",
    )(xconv, xconv, raw, taps, taps, dtb, alog)


def middle_kernel(
    index_ref, len_ref, summed_ref, v_ref, gate_ref, tok_ref, og_ref, gain_ref, skip_ref,
    own_ref, core_ref, up_ref, down_ref, cup_ref, cdown_ref,
    out_ref, m_ref, do_ref, dscan_ref, dgate_ref, rowsum_ref, sums_ref, dm_ref,
):
    me = index_ref[0]
    part = own_ref.shape[0]
    weights = [
        own_ref[...],
        core_ref[...],
        jnp.concatenate([up_ref[...], down_ref[...]], axis=0),
        jnp.concatenate([cup_ref[...], cdown_ref[...]], axis=0),
    ]
    channels = [pl.ds(pl.multiple_of((me ^ k) * part, part), part) for k in range(4)]
    step = pl.program_id(0)
    block = summed_ref.shape[0]
    per_slot = LEN // block
    count = len_ref[step // per_slot]
    row = lax.broadcasted_iota(jnp.int32, (block, 1), 0) + lax.rem(step, per_slot) * block
    live = row < count

    @pl.when(step == 0)
    def _():
        sums_ref[...] = jnp.zeros_like(sums_ref)

    summed = summed_ref[...]
    v = v_ref[...].astype(F32)
    gate = gate_ref[...]
    gain = gain_ref[...]
    skip = skip_ref[...]
    scanned = summed + skip * v
    sg = sigmoid(gate)
    act = gate * sg
    gated = scanned * act
    scale = lax.rsqrt(jnp.mean(gated * gated, axis=1, keepdims=True) + 1e-05)
    unit = gated * scale
    mixed = (unit * gain).astype(BF)
    m_ref[...] = mixed
    result = tok_ref[...].astype(F32)
    for lanes, weight in zip(channels, weights):
        result = result + dot(m_ref[:, lanes], weight)
    out_ref[...] = jnp.where(live, result, 0.0).astype(BF)
    dout = jnp.where(live, og_ref[...].astype(F32), 0.0).astype(BF)
    do_ref[...] = dout
    for lanes, weight in zip(channels, weights):
        dm_ref[:, lanes] = dot_nt(dout, weight)
    dmixed = dm_ref[...]
    sums_ref[0:1, :] += jnp.sum(dmixed * unit, axis=0, keepdims=True)
    dunit = dmixed * gain
    dgated = scale * (dunit - unit * jnp.mean(dunit * unit, axis=1, keepdims=True))
    dscan = dgated * act
    dscan_ref[...] = dscan
    dgate_ref[...] = (dgated * scanned * (sg * (1.0 + gate * (1.0 - sg)))).astype(BF)
    sums_ref[1:2, :] += jnp.sum(dscan * v, axis=0, keepdims=True)
    channel = lax.broadcasted_iota(jnp.int32, (INNER, 128), 0)
    lane = lax.broadcasted_iota(jnp.int32, (INNER, 128), 1)
    heads = jnp.where(channel // 64 == lane, 1.0, 0.0).astype(BF)
    rowsum_ref[...] = dot_split(dscan.astype(BF).astype(F32) * summed, heads)


def middle(index, lengths, summed, v, gate, tokens, out_grad, shards, gain, skip, block=128):
    rows = summed.shape[0]
    wide = pl.BlockSpec((block, INNER), lambda step, index, lens: (step, 0))
    narrow = pl.BlockSpec((block, D), lambda step, index, lens: (step, 0))
    vector = pl.BlockSpec((1, INNER), lambda step, index, lens: (0, 0))
    return pl.pallas_call(
        middle_kernel,
        grid_spec=pltpu.PrefetchScalarGridSpec(
            num_scalar_prefetch=2,
            grid=(rows // block,),
            in_specs=[wide, wide, wide, narrow, narrow, vector, vector]
            + [pl.BlockSpec(s.shape, lambda step, index, lens: (0, 0)) for s in shards],
            out_specs=[
                narrow, wide, narrow, wide, wide,
                pl.BlockSpec((block, 128), lambda step, index, lens: (step, 0)),
                pl.BlockSpec((8, INNER), lambda step, index, lens: (0, 0)),
            ],
            scratch_shapes=[pltpu.VMEM((block, INNER), F32)],
        ),
        out_shape=[
            jax.ShapeDtypeStruct((rows, D), BF),
            jax.ShapeDtypeStruct((rows, INNER), BF),
            jax.ShapeDtypeStruct((rows, D), BF),
            jax.ShapeDtypeStruct((rows, INNER), F32),
            jax.ShapeDtypeStruct((rows, INNER), BF),
            jax.ShapeDtypeStruct((rows, 128), F32),
            jax.ShapeDtypeStruct((8, INNER), F32),
        ],
        compiler_params=pltpu.CompilerParams(
            dimension_semantics=("arbitrary",), vmem_limit_bytes=VMEM_LIMIT
        ),
        name="middle",
    )(index, lengths, summed, v, gate, tokens, out_grad, gain, skip, *shards)


def scan_backward_kernel(
    xv_ref, xbc_ref, raw_ref, tv_ref, tbc_ref, dtb_ref, alog_ref, skip_ref,
    v_ref, bc_ref, step_ref, cum_ref, dscan_ref, rowsum_ref,
    dx_ref, dtaps_ref, dsmall_ref,
    st_ref, dst_ref, cumt_ref, colsum_ref,
):
    group = pl.program_id(1)

    @pl.when(group == 0)
    def _():
        bc = bc_ref[...]
        st_ref[...] = dot_nt(bc[:, :STATE], bc[:, STATE:])
        dst_ref[...] = jnp.zeros_like(dst_ref)
        colsum_ref[...] = jnp.zeros_like(colsum_ref)
        cumt_ref[...] = cum_ref[...].T

    shift = lax.rem(128 - GHEADS * group, 128)
    cum_cols = pltpu.roll(cum_ref[...], shift, axis=1)
    step_cols = pltpu.roll(step_ref[...], shift, axis=1)
    cum_rows = cumt_ref[pl.ds(pl.multiple_of(GHEADS * group, GHEADS), GHEADS), :]
    down, across = tri_masks()
    live = across >= down
    dvs = []
    for pair in range(GHEADS // 2):
        lanes = slice(128 * pair, 128 * pair + 128)
        vp = v_ref[:, lanes]
        dsp = dscan_ref[:, lanes].astype(BF)
        top = jnp.zeros((HALF, 128), F32)
        bottom = jnp.zeros((HALF, 128), F32)
        d00 = dst_ref[:HALF, :HALF]
        d01 = dst_ref[:HALF, HALF:]
        d11 = dst_ref[HALF:, HALF:]
        for side in range(2):
            head = 2 * pair + side
            vm = head_lanes(vp, side == 0)
            dsm = head_lanes(dsp, side == 0)
            ci = cum_rows[head : head + 1, :]
            cj = cum_cols[:, head : head + 1]
            sj = step_cols[:, head : head + 1]
            w00 = jnp.where(live, jnp.exp2(ci[:, :HALF] - cj[:HALF]), 0.0) * sj[:HALF]
            w01 = jnp.exp2(ci[:, HALF:] - cj[:HALF]) * sj[:HALF]
            w11 = jnp.where(live, jnp.exp2(ci[:, HALF:] - cj[HALF:]), 0.0) * sj[HALF:]
            dtop = dot_nt(vm[:HALF], dsp)
            dbottom = dot_nt(vm[HALF:], dsp[HALF:])
            d00 = d00 + dtop[:, :HALF] * w00
            d01 = d01 + dtop[:, HALF:] * w01
            d11 = d11 + dbottom * w11
            m00 = (st_ref[:HALF, :HALF] * w00).astype(BF)
            m01 = (st_ref[:HALF, HALF:] * w01).astype(BF)
            m11 = (st_ref[HALF:, HALF:] * w11).astype(BF)
            top = top + dot(jnp.concatenate([m00, m01], axis=1), dsm)
            bottom = bottom + dot(m11, dsm[HALF:])
        dst_ref[:HALF, :HALF] = d00
        dst_ref[:HALF, HALF:] = d01
        dst_ref[HALF:, HALF:] = d11
        dvs.append(jnp.concatenate([top, bottom], axis=0))
    dv = jnp.concatenate(dvs, axis=1)
    channel = lax.broadcasted_iota(jnp.int32, (GCOLS, 128), 0)
    lane = lax.broadcasted_iota(jnp.int32, (GCOLS, 128), 1)
    heads = jnp.where(channel // 64 + GHEADS * group == lane, 1.0, 0.0).astype(BF)
    colsum_ref[...] += dot_split(v_ref[...].astype(F32) * dv, heads)
    dact = dv + skip_ref[...] * dscan_ref[...]
    columns = pl.ds(pl.multiple_of(GCOLS * group, GCOLS), GCOLS)
    dx = conv_backward(
        xv_ref[...], tv_ref[0:4, :], tv_ref[4:5, :], dact, dtaps_ref, columns
    )
    dx_ref[:, columns] = dx.astype(BF)

    @pl.when(group == GROUPS - 1)
    def _():
        bc = bc_ref[...]
        dst = dst_ref[...].astype(BF)
        db = dot(dst, bc[:, STATE:])
        dc = dot_tn(dst, bc[:, :STATE])
        dbc = conv_backward(
            xbc_ref[...], tbc_ref[0:4, :], tbc_ref[4:5, :],
            jnp.concatenate([db, dc], axis=1), dtaps_ref, slice(INNER, CONVCH),
        )
        dx_ref[:, INNER:CONVCH] = dbc.astype(BF)
        row = lax.broadcasted_iota(jnp.int32, (LEN, LEN), 0)
        col = lax.broadcasted_iota(jnp.int32, (LEN, LEN), 1)
        upper = jnp.where(col >= row, 1.0, 0.0).astype(BF)
        colsum = colsum_ref[...]
        dlog = dot_exact(upper, rowsum_ref[...] - colsum)
        step = step_ref[...]
        rate = jnp.exp(alog_ref[...])
        z = raw_ref[...] + dtb_ref[...]
        sg = 1.0 / (1.0 + jnp.exp(-z))
        tiny = z < -20.0
        ratio = jnp.where(tiny, 1.0, sg / jnp.where(tiny, 1.0, step))
        draw = colsum * ratio - dlog * rate * sg
        lane32 = lax.broadcasted_iota(jnp.int32, (LEN, 128), 1)
        draw = jnp.where(lane32 < HEADS, draw, 0.0)
        dx_ref[:, CONVCH:] = draw.astype(BF)
        dalog = -dlog * step * rate
        dsmall_ref[0] = jnp.concatenate(
            [
                jnp.sum(draw, axis=0, keepdims=True),
                jnp.sum(dalog, axis=0, keepdims=True),
                jnp.zeros((6, 128), F32),
            ],
            axis=0,
        )


def scan_backward(xconv, raw, taps, dtb, alog, skip, v, bc, step, cum, dscan, rowsum, slots):
    rows = slots * LEN
    by_slot = lambda slot, group: (slot, 0)
    fixed = lambda slot, group: (0, 0)
    by_group = pl.BlockSpec((LEN, GCOLS), lambda slot, group: (slot, group))
    last = INNER // (2 * STATE)
    return pl.pallas_call(
        scan_backward_kernel,
        grid=(slots, GROUPS),
        in_specs=[
            by_group,
            pl.BlockSpec((LEN, 2 * STATE), lambda slot, group: (slot, last)),
            pl.BlockSpec((LEN, 128), by_slot),
            pl.BlockSpec((8, GCOLS), lambda slot, group: (0, group)),
            pl.BlockSpec((8, 2 * STATE), lambda slot, group: (0, last)),
            pl.BlockSpec((1, 128), fixed),
            pl.BlockSpec((1, 128), fixed),
            pl.BlockSpec((1, GCOLS), lambda slot, group: (0, group)),
            by_group,
            pl.BlockSpec((LEN, 2 * STATE), by_slot),
            pl.BlockSpec((LEN, 128), by_slot),
            pl.BlockSpec((LEN, 128), by_slot),
            by_group,
            pl.BlockSpec((LEN, 128), by_slot),
        ],
        out_specs=[
            pl.BlockSpec((LEN, CONVCH + 128), by_slot),
            pl.BlockSpec((1, 8, CONVCH), lambda slot, group: (slot, 0, 0)),
            pl.BlockSpec((1, 8, 128), lambda slot, group: (slot, 0, 0)),
        ],
        out_shape=[
            jax.ShapeDtypeStruct((rows, CONVCH + 128), BF),
            jax.ShapeDtypeStruct((slots, 8, CONVCH), F32),
            jax.ShapeDtypeStruct((slots, 8, 128), F32),
        ],
        scratch_shapes=[
            pltpu.VMEM((LEN, LEN), F32),
            pltpu.VMEM((LEN, LEN), F32),
            pltpu.VMEM((128, LEN), F32),
            pltpu.VMEM((LEN, 128), F32),
        ],
        compiler_params=pltpu.CompilerParams(
            dimension_semantics=("arbitrary", "arbitrary"), vmem_limit_bytes=VMEM_LIMIT
        ),
        name="scan_backward",
    )(xconv, xconv, raw, taps, taps, dtb, alog, skip, v, bc, step, cum, dscan, rowsum)


def project_kernel(index_ref, n_ref, own_ref, core_ref, up_ref, down_ref, cup_ref, cdown_ref, out_ref):
    me = index_ref[0]
    part = own_ref.shape[0]

    def columns(k):
        return n_ref[:, pl.ds(pl.multiple_of((me ^ k) * part, part), part)]

    out_ref[...] = (
        dot(columns(0), own_ref[...])
        + dot(columns(1), core_ref[...])
        + dot(columns(2), jnp.concatenate([up_ref[...], down_ref[...]], axis=0))
        + dot(columns(3), jnp.concatenate([cup_ref[...], cdown_ref[...]], axis=0))
    )


def project(index, normed, shards, block):
    rows = normed.shape[0]
    columns = shards[0].shape[1]
    return pl.pallas_call(
        project_kernel,
        grid_spec=pltpu.PrefetchScalarGridSpec(
            num_scalar_prefetch=1,
            grid=(columns // block,),
            in_specs=[pl.BlockSpec(normed.shape, lambda step, index: (0, 0))]
            + [pl.BlockSpec((s.shape[0], block), lambda step, index: (0, step)) for s in shards],
            out_specs=pl.BlockSpec((rows, block), lambda step, index: (0, step)),
        ),
        out_shape=jax.ShapeDtypeStruct((rows, columns), F32),
        compiler_params=pltpu.CompilerParams(
            dimension_semantics=("arbitrary",), vmem_limit_bytes=VMEM_LIMIT
        ),
        name="project",
    )(index, normed, *shards)


def input_grad_kernel(index_ref, tok_ref, do_ref, dgate_ref, dx_ref, gain_ref, wstep_ref, *refs):
    gate_refs, conv_refs = refs[0:6], refs[6:12]
    out_ref, dgain_ref, dn_ref = refs[12:15]
    me = index_ref[0]
    part = gate_refs[0].shape[0]
    dgate = dgate_ref[...]
    dconv = dx_ref[:, :CONVCH]
    draw = dx_ref[:, CONVCH:]

    @pl.when(pl.program_id(0) == 0)
    def _():
        dgain_ref[...] = jnp.zeros_like(dgain_ref)

    def pieces(refs):
        return [
            refs[0][...],
            refs[1][...],
            jnp.concatenate([refs[2][...], refs[3][...]], axis=0),
            jnp.concatenate([refs[4][...], refs[5][...]], axis=0),
        ]

    for k, (wg, wc) in enumerate(zip(pieces(gate_refs), pieces(conv_refs))):
        lanes = pl.ds(pl.multiple_of((me ^ k) * part, part), part)
        dn_ref[:, lanes] = (
            dot_nt(dgate, wg) + dot_nt(dconv, wc) + dot(draw, wstep_ref[:, lanes])
        )
    dn = dn_ref[...]
    x = tok_ref[...].astype(F32)
    scale = lax.rsqrt(jnp.mean(x * x, axis=1, keepdims=True) + 1e-05)
    unit = x * scale
    dgain_ref[0:1, :] += jnp.sum(dn * unit, axis=0, keepdims=True)
    dunit = dn * gain_ref[...]
    out_ref[...] = do_ref[...].astype(F32) + scale * (
        dunit - unit * jnp.mean(dunit * unit, axis=1, keepdims=True)
    )


def input_grad(index, tokens, dout, dgate, dx, gain, wstep_t, gate_shards, conv_shards, block=128):
    rows = tokens.shape[0]
    by_row = lambda v: pl.BlockSpec((block, v.shape[1]), lambda step, index: (step, 0))
    whole = lambda v: pl.BlockSpec(v.shape, lambda step, index: (0, 0))
    shards = list(gate_shards) + list(conv_shards)
    return pl.pallas_call(
        input_grad_kernel,
        grid_spec=pltpu.PrefetchScalarGridSpec(
            num_scalar_prefetch=1,
            grid=(rows // block,),
            in_specs=[by_row(v) for v in (tokens, dout, dgate, dx)]
            + [whole(v) for v in [gain, wstep_t] + shards],
            out_specs=[by_row(tokens), pl.BlockSpec((8, D), lambda step, index: (0, 0))],
            scratch_shapes=[pltpu.VMEM((block, D), F32)],
        ),
        out_shape=[
            jax.ShapeDtypeStruct((rows, D), F32),
            jax.ShapeDtypeStruct((8, D), F32),
        ],
        compiler_params=pltpu.CompilerParams(
            dimension_semantics=("arbitrary",), vmem_limit_bytes=VMEM_LIMIT
        ),
        name="input_grad",
    )(index, tokens, dout, dgate, dx, gain, wstep_t, *shards)


SWAP = [(0, 1), (1, 0)]
RING = 4


def y_shift(by):
    place = lambda y: (y % 2) * 2 + y // 2
    return [(place(y), place((y + by) % 4)) for y in range(4)]


def shift(by):
    return [(i, (i + by) % RING) for i in range(RING)]


def take_shards(shard):
    half = shard.shape[0] // 2
    core = lax.ppermute(shard, "core", SWAP)
    up = lax.ppermute(shard[:half], ("yl", "yh"), y_shift(1))
    down = lax.ppermute(shard[half:], ("yl", "yh"), y_shift(-1))
    cup = lax.ppermute(up, "core", SWAP)
    cdown = lax.ppermute(down, "core", SWAP)
    return (shard, core, up, down, cup, cdown)


def after(values, *others):
    return lax.optimization_barrier((values,) + others)[0]


def scatter_rows(part, axis):
    quarter = part.shape[1] // RING
    me = lax.axis_index(axis)

    def rows(owner):
        return lax.dynamic_slice_in_dim(part, owner * quarter, quarter, axis=1)

    total = rows(me).astype(F32)
    got = [
        lax.ppermute(rows(lax.rem(me + by, RING)), axis, shift(by)) for by in range(1, RING)
    ]
    for piece in got:
        total = total + piece.astype(F32)
    return total.astype(BF)


def gather_rows(part, axis):
    me = lax.axis_index(axis)
    got = [part] + [lax.ppermute(part, axis, shift(by)) for by in range(RING - 1, 0, -1)]
    stacked = jnp.stack(got, axis=0)
    return jnp.roll(stacked, me, axis=0).reshape((-1,) + part.shape[1:])


def sum_y(part):
    yl = lax.axis_index("yl")
    own = lax.dynamic_index_in_dim(part, yl, 0, keepdims=False)
    other = lax.dynamic_index_in_dim(part, 1 - yl, 0, keepdims=False)
    right = lax.ppermute(other, ("yl", "yh"), y_shift(1))
    left = lax.ppermute(other, ("yl", "yh"), y_shift(-1))
    across = lax.ppermute(own, "yh", SWAP)
    f = lambda v: v.astype(F32)
    return ((f(own) + f(across)) + (f(left) + f(right))).astype(BF)


def sum_core(grad):
    core = lax.axis_index("core")
    own = lax.dynamic_index_in_dim(grad, core, 1, keepdims=False)
    other = lax.dynamic_index_in_dim(grad, 1 - core, 1, keepdims=False)
    got = lax.ppermute(other, "core", SWAP)
    return (own.astype(F32) + got.astype(F32)).astype(BF)


def reduce_weight(grad):
    rows = grad.shape[0] // 4
    columns = grad.shape[1]
    cut = (columns // 256) * 128
    half = sum_core(grad.reshape(2, 2, rows, columns))
    outs = []
    for part, axes in ((half[..., :cut], ("x", "z")), (half[..., cut:], ("z", "x"))):
        part = scatter_rows(scatter_rows(part, axes[0]), axes[1])
        part = sum_y(part)
        outs.append(gather_rows(gather_rows(part, axes[1]), axes[0]))
    return jnp.concatenate(outs, axis=1).astype(F32)


def reduce_small(vector):
    total = sum_core(vector.astype(BF).reshape(2, 2, *vector.shape[1:]))
    for axis in ("x", "z"):
        got = [lax.ppermute(total, axis, shift(by)) for by in range(1, RING)]
        f = lambda v: v.astype(F32)
        total = ((f(total) + f(got[1])) + (f(got[0]) + f(got[2]))).astype(BF)
    return sum_y(total).astype(F32)


SMALL = (D // 4, CONV * CONVCH // 4, CONVCH // 4, HEADS // 4, HEADS // 4, HEADS // 4, INNER // 4, D // 4 * HEADS)
SMALL_ROWS = 96


def pack(pieces):
    flat = jnp.concatenate(pieces, axis=-1)
    pad = SMALL_ROWS * 128 - flat.shape[-1]
    flat = jnp.pad(flat, [(0, 0)] * (flat.ndim - 1) + [(0, pad)])
    return flat.reshape(flat.shape[:-1] + (SMALL_ROWS, 128))


def unpack(packed):
    flat = packed.reshape(packed.shape[:-2] + (-1,))
    out, at = [], 0
    for size in SMALL:
        out.append(flat[..., at : at + size])
        at += size
    return out


def local(
    tokens, norm_gain, in_proj, conv_weight, conv_bias, dt_bias, a_log, d_skip, gate_gain,
    out_proj, out_grad, lengths,
):
    slots = lengths.shape[0]
    me = lax.axis_index("yl") * 2 + lax.axis_index("core")
    index = me[None].astype(jnp.int32)

    packed = pack(
        [
            norm_gain, conv_weight.reshape(-1), conv_bias, dt_bias, a_log, d_skip, gate_gain,
            in_proj[:, INNER + CONVCH :].reshape(-1),
        ]
    )
    own, core, up, down, cup, cdown = take_shards(packed)
    relative = jnp.stack(
        [own, core, jnp.concatenate([up, down]), jnp.concatenate([cup, cdown])]
    )
    order = jnp.arange(4) ^ me
    whole = unpack(jnp.take(relative, order, axis=0))
    f = lambda v: v.astype(F32)
    gain = f(whole[0]).reshape(1, D)
    conv_w = f(whole[1]).reshape(4, CONV, CONVCH // 4).transpose(1, 0, 2).reshape(CONV, CONVCH)
    taps = jnp.concatenate(
        [conv_w, f(whole[2]).reshape(1, CONVCH), jnp.zeros((3, CONVCH), F32)], axis=0
    )
    pad = lambda v: jnp.pad(f(v).reshape(1, HEADS), ((0, 0), (0, 128 - HEADS)))
    dtb, alog = pad(whole[3]), pad(whole[4])
    skip = jnp.repeat(f(whole[5]).reshape(HEADS), INNER // HEADS)[None, :]
    gate_gain_all = f(whole[6]).reshape(1, INNER)
    wstep = jnp.pad(whole[7].reshape(D, HEADS), ((0, 0), (0, 128 - HEADS)))

    conv_shards = take_shards(in_proj[:, INNER : INNER + CONVCH])
    gate_shards = take_shards(after(in_proj[:, :INNER], conv_shards[2], conv_shards[3]))
    out_shards = take_shards(after(out_proj, gate_shards[2], gate_shards[3]))

    x = tokens.astype(F32)
    scale = lax.rsqrt(jnp.mean(x * x, axis=1, keepdims=True) + 1e-05)
    normed = lax.optimization_barrier((x * scale * gain).astype(BF))
    raw = dot(normed, wstep)
    xconv = project(index, normed, conv_shards, 768)
    summed, v, bc, step, cum = scan_forward(xconv, raw, taps, dtb, alog, slots)
    gate = project(index, normed, gate_shards, 512)
    block_out, mixed, dout, dscan, dgate, rowsum, sums = middle(
        index, lengths, summed, v, gate, tokens, out_grad, out_shards, gate_gain_all, skip
    )
    g_out = reduce_weight(dot_tn(mixed, dout).astype(BF))
    g_gate = reduce_weight(dot_tn(normed, dgate).astype(BF))
    dx, dtaps, dsmall = scan_backward(
        xconv, raw, taps, dtb, alog, skip, v, bc, step, cum, dscan, rowsum, slots
    )
    d_in = dot_tn(normed, dx)
    g_conv = reduce_weight(d_in[:, :CONVCH].astype(BF))
    tokens_grad, dgain = input_grad(
        index, tokens, dout, dgate, dx, gain, wstep.T, gate_shards, conv_shards
    )
    dtaps = jnp.sum(dtaps, axis=0)
    dsmall = jnp.sum(dsmall, axis=0)
    d_skip = jnp.sum(sums[1].reshape(HEADS, INNER // HEADS), axis=1)
    four = lambda v: v.reshape(4, -1)
    small = reduce_small(
        pack(
            [
                four(dgain[0]),
                dtaps[0:4].reshape(CONV, 4, CONVCH // 4).transpose(1, 0, 2).reshape(4, -1),
                four(dtaps[4]), four(dsmall[0, :HEADS]), four(dsmall[1, :HEADS]), four(d_skip),
                four(sums[0]), four(d_in[:, CONVCH : CONVCH + HEADS]),
            ]
        )
    )
    s_gain, s_taps, s_bias, s_dtb, s_alog, s_skip, s_gate, s_step = unpack(small)
    return (
        block_out,
        tokens_grad,
        s_gain,
        jnp.concatenate([g_gate, g_conv, s_step.reshape(D // 4, HEADS)], axis=1),
        s_taps.reshape(CONV, CONVCH // 4),
        s_bias, s_dtb, s_alog, s_skip, s_gate,
        g_out,
    )


def solution(mesh):
    names = ("yl", "core", "z", "x", "yh")
    fine = Mesh(mesh.devices.reshape(2, 2, 4, 4, 2), names)
    every = P(names, None)
    shard = P(("yl", "core"))
    rows = P(("yl", "core"), None)
    columns = P(None, ("yl", "core"))
    return jax.shard_map(
        local,
        mesh=fine,
        in_specs=(
            every, shard, rows, columns, shard, shard, shard, shard, shard, rows, every, P(names),
        ),
        out_specs=(
            every, every, shard, rows, columns, shard, shard, shard, shard, shard, rows,
        ),
        check_vma=False,
    )
```

time: 931 us -> 413 us (0.44)
  waiting for transfers between devices: 343 us -> 56.7 us
  blocking collectives: 217 us -> 0 us
  starting transfers between devices: 0.24 us -> 176 us
  other arithmetic: 145 us -> 22.7 us
  matrix products: 117 us -> 14.4 us
  Pallas kernels: 0 us -> 84.7 us
  loops' own time: 28.9 us -> 0 us
  between operations: 18.1 us -> 2.21 us
    psum x1 -> x0, blocking collectives: 183 us -> none  [local(): lax.psum(s_norm.astype(jnp.bfloat16), 'dp').astype(jnp.float32)]
    ppermute x0 -> x123, starting transfers between devices: none -> 176 us  [the longest x36 53 us: scatter_rows(): lax.ppermute(rows(lax.rem(me + by, RING)), axis, shift(by))]
    psum x1 -> x0, waiting for transfers between devices: 119 us -> none  [local(): lax.psum(s_inproj.astype(jnp.bfloat16), 'dp').astype(jnp.float32)]
    reduce_scatter x2 -> x0, waiting for transfers between devices: 118 us -> none  [the longest x1 87.3 us: local(): lax.psum_scatter(g_inproj.astype(jnp.bfloat16), 'fsdp', scatter_dimension...]
    all_gather x2 -> x0, waiting for transfers between devices: 106 us -> none  [the longest x1 91.1 us: local(): lax.all_gather(in_proj, 'fsdp', axis=0, tiled=True)]
    dot_general x30 -> x4, matrix products: 117 us -> 14.4 us  [the longest x3 14 us: dot_tn(): lax.dot_general(a, b, (((0,), (0,)), ((), ())), preferred_element_type=F32)]
    pallas_call x0 -> x6, Pallas kernels: none -> 84.7 us  [the longest x1 21.8 us: middle(): pl.pallas_call(middle_kernel, grid_spec=pltpu.PrefetchScalarGridSpec(num_...]
    ppermute x0 -> x123, waiting for transfers between devices: none -> 56.7 us  [the longest x36 19.3 us: scatter_rows(): lax.ppermute(rows(lax.rem(me + by, RING)), axis, shift(by))]
  transfers between devices with their start and end apart: 6 -> 123, of which waited for: 5 -> 28; matrix products, arithmetic and copies ran while one was open for 10% -> 12% of each run, Pallas kernels for 0% -> 6%
where the time goes in v1:
time: 413 us; the launch traced here: 405 us
  starting transfers between devices  176 us (43%)
  Pallas kernels  84.7 us (21%)
  waiting for transfers between devices  56.7 us (14%)
  local copies, waits for them, and re-layouts  48.9 us (12%)
  other arithmetic  22.7 us (5%)
  matrix products  14.4 us (3%)
    ppermute x36, starting transfers between devices, scatter_rows(): lax.ppermute(rows(lax.rem(me + by, RING)), axis, shift(by))  53 us
    ppermute x36, starting transfers between devices, gather_rows(): lax.ppermute(part, axis, shift(by))  52.2 us
    ppermute x7, starting transfers between devices, sum_y(): across = lax.ppermute(own, 'yh', SWAP)  29.8 us
    pallas_call x1, Pallas kernels, middle(): pl.pallas_call(middle_kernel, grid_spec=pltpu.PrefetchScalarGridSpec(num_...  21.8 us
    pallas_call x1, Pallas kernels, scan_backward(): pl.pallas_call(scan_backward_kernel, grid=(slots, GROUPS), in_specs=[by_g...  20.8 us
    ppermute x36, waiting for transfers between devices, scatter_rows(): lax.ppermute(rows(lax.rem(me + by, RING)), axis, shift(by))  19.3 us
    unnamed x63, local copies, waits for them, and re-layouts  18.2 us
    pallas_call x1, Pallas kernels, input_grad(): pl.pallas_call(input_grad_kernel, grid_spec=pltpu.PrefetchScalarGridSpec(...  18.1 us
  transfers between devices with their start and end apart: 123, of which 28 were waited for; matrix products, arithmetic and copies ran while one was open for 12% of the time, Pallas kernels for 6%

profile of v1, /device:TPU:8, one launch (start us, length us, event | category | flops | bytes accessed | tf_op | source)
XLA Modules:
  0.0 405.2 jit_solution(14896467430345032589)
XLA Ops:
  2.4 4.1 %concatenate.46 = bf16[11864]{0:T(1024)(128)(2,1)S(1)} concatenate(bf16[256]{0:T(256)(128)(2,1)} %param.25, bf16[2304]{0:T(1024)(128)(2,1)S(1)} %reshape.201, bf16[576]{0:T(1024)(128)(2,1)} %param.28, bf16[8]{0:T(256)(128)(2,1)} %param.29, bf16[8]{0:T(256)(128)(2,1)} %param.30, bf16[8]{0:T(256)(128)(2,1)} %param.31, bf16[512]{0:T(512)(128)(2,1)} %param.32, ...), dimensions={0} | concatenate | bytes 47456 | tf_op jit(solution)/shard_map/concatenate | solution.py:645
  21.9 5.2 %collective-permute-done.6.up_ref.refs_8_ = bf16[128,2304]{1,0:T(8,128)(2,1)S(1)} collective-permute-done((bf16[128,2304]{1,0:T(8,128)(2,1)}, bf16[128,2304]{1,0:T(8,128)(2,1)S(1)}, u32[]{:S(2)}, u32[]{:S(2)}) %collective-permute-start.6) | collective-permute-done | bytes 589856 | tf_op jit(solution)/shard_map/ppermute | solution.py:565
  34.4 8.4 %collective-permute-done.11.up_ref.refs_2_ = bf16[128,2048]{1,0:T(8,128)(2,1)} collective-permute-done((bf16[128,2048]{1,0:T(8,128)(2,1)S(1)}, bf16[128,2048]{1,0:T(8,128)(2,1)}, u32[]{:S(2)}, u32[]{:S(2)}) %collective-permute-start.11) | collective-permute-done | bytes 524320 | tf_op jit(solution)/shard_map/ppermute | solution.py:565
  60.5 6.0 %project.2.xv_ref.xbc_ref = f32[512,2304]{1,0:T(8,128)} custom-call(s32[1]{0:T(128)} %bitcast.index_ref, bf16[512,1024]{1,0:T(8,128)(2,1)S(1)} %fusion.5.n_ref, bf16[256,2304]{1,0:T(8,128)(2,1)} %copy.54.own_ref.refs_6_, bf16[256,2304]{1,0:T(8,128)(2,1)} %collective-permute-done.5.core_ref.refs_7_, ...), custom_call_target="tpu_custom_call" | custom-call | tf_op jit(solution)/shard_map/project/pallas_call | solution.py:469
  66.5 12.1 %scan_forward.1 = (f32[512,2048]{1,0:T(8,128)}, bf16[512,2048]{1,0:T(8,128)(2,1)S(1)}, bf16[512,256]{1,0:T(8,128)(2,1)S(1)}, f32[512,128]{1,0:T(8,128)S(1)}, f32[512,128]{1,0:T(8,128)S(1)}) custom-call(f32[512,2304]{1,0:T(8,128)} %project.2.xv_ref.xbc_ref, f32[512,2304]{1,0:T(8,128)} %project.2.xv_ref.xbc_ref, f32[512,128]{1,0:T(8,128)S(1)} %fusion.48.raw_ref, ...), custom_call_target="tpu_custom_call" | custom-call | tf_op jit(solution)/shard_map/scan_forward/pallas_call | solution.py:165
  80.9 5.9 %project.3.gate_ref = f32[512,2048]{1,0:T(8,128)} custom-call(s32[1]{0:T(128)} %bitcast.index_ref, bf16[512,1024]{1,0:T(8,128)(2,1)S(1)} %fusion.5.n_ref, bf16[256,2048]{1,0:T(8,128)(2,1)} %copy-done.13, bf16[256,2048]{1,0:T(8,128)(2,1)} %copy-done.19, bf16[128,2048]{1,0:T(8,128)(2,1)} %collective-permute-done.11.up_ref.refs_2_, ...), custom_call_target="tpu_custom_call" | custom-call | tf_op jit(solution)/shard_map/project/pallas_call | solution.py:469
  87.9 21.8 %middle.1 = (bf16[512,1024]{1,0:T(8,128)(2,1)}, bf16[512,2048]{1,0:T(8,128)(2,1)}, bf16[512,1024]{1,0:T(8,128)(2,1)S(1)}, f32[512,2048]{1,0:T(8,128)}, bf16[512,...) custom-call(s32[1]{0:T(128)} %bitcast.index_ref, s32[2]{0:T(128)S(1)} %copy-done.10, ...), custom_call_target="tpu_custom_call" | custom-call | tf_op jit(solution)/shard_map/middle/pallas_call | solution.py:268
  110.6 20.8 %scan_backward.1 = (bf16[512,2432]{1,0:T(8,128)(2,1)}, f32[2,8,2304]{2,1,0:T(8,128)S(1)}, f32[2,8,128]{2,1,0:T(8,128)S(1)}) custom-call(f32[512,2304]{1,0:T(8,128)} %project.2.xv_ref.xbc_ref, f32[512,2304]{1,0:T(8,128)} %project.2.xv_ref.xbc_ref, f32[512,128]{1,0:T(8,128)S(1)} %fusion.48.raw_ref, f32[8,2304]{1,0:T(8,128)S(1)} %maximum_maximum_fusion.tv_ref.tbc_ref, ...), custom_call_target="tpu_custom_call" | custom-call | tf_op jit(solution)/shard_map/scan_backward/pallas_call | solution.py:409
  131.6 5.3 %convolution_convert_fusion = bf16[1024,2432]{1,0:T(8,128)(2,1)S(1)} fusion(bf16[512,1024]{1,0:T(8,128)(2,1)S(1)} %fusion.5.n_ref, bf16[512,2432]{1,0:T(8,128)(2,1)} %get-tuple-element.48.dx_ref), kind=kOutput, calls=%fused_computation.1 | convolution fusion | flops 2552627200 | bytes 8519680 | tf_op jit(solution)/shard_map/dot_general | solution.py:35
  139.5 6.4 %convolution_convert_fusion.1 = bf16[2048,1024]{1,0:T(8,128)(2,1)} fusion(bf16[512,2048]{1,0:T(8,128)(2,1)} %get-tuple-element.54, bf16[512,1024]{1,0:T(8,128)(2,1)} %copy-done.9), kind=kOutput, calls=%fused_computation.9 | convolution fusion | flops 2149580800 | bytes 7340032 | tf_op jit(solution)/shard_map/dot_general | solution.py:35
  145.9 18.1 %input_grad.1 = (f32[512,1024]{1,0:T(8,128)}, f32[8,1024]{1,0:T(8,128)S(1)}) custom-call(s32[1]{0:T(128)} %bitcast.index_ref, bf16[512,1024]{1,0:T(8,128)(2,1)} %tok_ref.3, bf16[512,1024]{1,0:T(8,128)(2,1)} %copy-done.9, bf16[512,2048]{1,0:T(8,128)(2,1)} %get-tuple-element.42.dgate_ref, bf16[512,2432]{1,0:T(8,128)(2,1)} %get-tuple-element.48.dx_ref, ...), custom_call_target="tpu_custom_call" | custom-call | tf_op jit(solution)/shard_map/input_grad/pallas_call | solution.py:528
  177.9 4.0 collective-permute-start.24
  189.4 4.3 %collective-permute-start.27 = (bf16[96,128]{1,0:T(8,128)(2,1)S(1)}, bf16[96,128]{1,0:T(8,128)(2,1)S(1)}, u32[]{:S(2)}, u32[]{:S(2)}) collective-permute-start(bf16[96,128]{1,0:T(8,128)(2,1)S(1)} %get-tuple-element.136), channel_id=1, source_target_pairs={{0,1},{1,0},{2,3},{3,2},{4,5},{5,4},{6,7},{7,6},{8,9},{9,8},{10,11... | collective-permute-start | bytes 73736 | tf_op jit(solution)/shard_map/ppermute | solution.py:605
  202.4 4.3 %collective-permute-start.94 = (bf16[2,128,512]{2,1,0:T(8,128)(2,1)S(1)}, bf16[2,128,512]{2,1,0:T(8,128)(2,1)S(1)}, u32[]{:S(2)}, u32[]{:S(2)}) collective-permute-start(bf16[2,128,512]{2,1,0:T(8,128)(2,1)S(1)} %get-tuple-element.84), channel_id=1, source_target_pairs={{0,4},{2,6},{4,0},{6,2},{1,5},{3,7},{5,1},{7,3},{8,12},{10,14},{12... | collective-permute-start | bytes 786440 | tf_op jit(solution)/shard_map/ppermute | solution.py:585
  210.0 4.6 %collective-permute-start.109 = (bf16[2,128,512]{2,1,0:T(8,128)(2,1)S(1)}, bf16[2,128,512]{2,1,0:T(8,128)(2,1)S(1)}, u32[]{:S(2)}, u32[]{:S(2)}) collective-permute-start(bf16[2,128,512]{2,1,0:T(8,128)(2,1)S(1)} %get-tuple-element.87), channel_id=1, source_target_pairs={{0,16},{8,24},{16,0},{24,8},{1,17},{9,25},{17,1},{25,9},{2,18},{10... | collective-permute-start | bytes 786440 | tf_op jit(solution)/shard_map/ppermute | solution.py:585
  227.5 6.3 %collective-permute-done.31 = bf16[2,64,1024]{2,1,0:T(8,128)(2,1)S(1)} collective-permute-done((bf16[2,64,1024]{2,1,0:T(8,128)(2,1)S(1)}, bf16[2,64,1024]{2,1,0:T(8,128)(2,1)S(1)}, u32[]{:S(2)}, u32[]{:S(2)}) %collective-permute-start.31) | collective-permute-done | bytes 262176 | tf_op jit(solution)/shard_map/ppermute | solution.py:585
  261.0 5.3 %collective-permute-start.99 = (bf16[32,512]{1,0:T(8,128)(2,1)S(1)}, bf16[32,512]{1,0:T(8,128)(2,1)S(1)}, u32[]{:S(2)}, u32[]{:S(2)}) collective-permute-start(bf16[32,512]{1,0:T(8,128)(2,1)S(1)} %get-tuple-element.125), channel_id=1, source_target_pairs={{0,1},{1,0},{2,3},{3,2},{4,5},{5,4},{6,7},{7,6},{8,9},{9,8},{10,11... | collective-permute-start | bytes 98312 | tf_op jit(solution)/shard_map/ppermute | solution.py:605
  275.9 4.6 %collective-permute-start.37 = (bf16[16,1024]{1,0:T(8,128)(2,1)S(1)}, bf16[16,1024]{1,0:T(8,128)(2,1)S(1)}, u32[]{:S(2)}, u32[]{:S(2)}) collective-permute-start(bf16[16,1024]{1,0:T(8,128)(2,1)S(1)} %get-tuple-element.129), channel_id=1, source_target_pairs={{0,1},{1,0},{2,3},{3,2},{4,5},{5,4},{6,7},{7,6},{8,9},{9,8},{10,11... | collective-permute-start | bytes 98312 | tf_op jit(solution)/shard_map/ppermute | solution.py:605
  298.7 3.9 collective-permute-done.41
  319.7 4.3 %collective-permute-start.43 = (bf16[64,1024]{1,0:T(8,128)(2,1)S(1)}, bf16[64,1024]{1,0:T(8,128)(2,1)S(1)}, u32[]{:S(2)}, u32[]{:S(2)}) collective-permute-start(bf16[64,1024]{1,0:T(8,128)(2,1)S(1)} %bitcast.189), channel_id=1, source_target_pairs={{0,6},{2,0},{4,2},{6,4},{1,7},{3,1},{5,3},{7,5},{8,14},{10,8},{12,... | collective-permute-start | bytes 393224 | tf_op jit(solution)/shard_map/ppermute | solution.py:594
  339.5 4.8 %collective-permute-start.78 = (bf16[2,64,1152]{2,1,0:T(8,128)(2,1)S(1)}, bf16[2,64,1152]{2,1,0:T(8,128)(2,1)S(1)}, u32[]{:S(2)}, u32[]{:S(2)}) collective-permute-start(bf16[2,64,1152]{2,1,0:T(8,128)(2,1)S(1)} %get-tuple-element.81), channel_id=1, source_target_pairs={{0,16},{8,24},{16,0},{24,8},{1,17},{9,25},{17,1},{25,9},{2,18},{10... | collective-permute-start | bytes 884744 | tf_op jit(solution)/shard_map/ppermute | solution.py:585
  359.0 5.5 %collective-permute-start.68 = (bf16[16,1152]{1,0:T(8,128)(2,1)S(1)}, bf16[16,1152]{1,0:T(8,128)(2,1)S(1)}, u32[]{:S(2)}, u32[]{:S(2)}) collective-permute-start(bf16[16,1152]{1,0:T(8,128)(2,1)S(1)} %get-tuple-element.121), channel_id=1, source_target_pairs={{0,1},{1,0},{2,3},{3,2},{4,5},{5,4},{6,7},{7,6},{8,9},{9,8},{10,11... | collective-permute-start | bytes 110600 | tf_op jit(solution)/shard_map/ppermute | solution.py:605
  370.0 5.6 %collective-permute-start.71 = (bf16[16,1152]{1,0:T(8,128)(2,1)S(1)}, bf16[16,1152]{1,0:T(8,128)(2,1)S(1)}, u32[]{:S(2)}, u32[]{:S(2)}) collective-permute-start(bf16[16,1152]{1,0:T(8,128)(2,1)S(1)} %add_convert_fusion.15), channel_id=1, source_target_pairs={{0,24},{8,0},{16,8},{24,16},{1,25},{9,1},{17,9},{25,17},{2,26},{10... | collective-permute-start | bytes 110600 | tf_op jit(solution)/shard_map/ppermute | solution.py:594
  399.1 5.9 %copy.53 = f32[256,4384]{0,1:T(8,128)} copy(f32[256,4384]{1,0:T(8,128)} %pad_maximum_fusion) | data formatting | bytes 8978432
  (443 shorter events, 225.7 us)
Async XLA Ops:
  11.2 15.9 %collective-permute-start.6 = (bf16[128,2304]{1,0:T(8,128)(2,1)}, bf16[128,2304]{1,0:T(8,128)(2,1)S(1)}, u32[]{:S(2)}, u32[]{:S(2)}) collective-permute-start(bf16[128,2304]{1,0:T(8,128)(2,1)} %copy.55), channel_id=1, source_target_pairs={{0,64},{64,1},{1,65},{65,0},{2,66},{66,3},{3,67},{67,2},{4,68},{68... | collective-permute-start | bytes 1769480 | tf_op jit(solution)/shard_map/ppermute | solution.py:565
  13.8 15.6 %collective-permute-start.7 = (bf16[128,2304]{1,0:T(8,128)(2,1)}, bf16[128,2304]{1,0:T(8,128)(2,1)S(1)}, u32[]{:S(2)}, u32[]{:S(2)}) collective-permute-start(bf16[128,2304]{1,0:T(8,128)(2,1)} %copy.56), channel_id=1, source_target_pairs={{0,65},{64,0},{1,64},{65,1},{2,67},{66,2},{3,66},{67,3},{4,69},{68... | collective-permute-start | bytes 1769480 | tf_op jit(solution)/shard_map/ppermute | solution.py:566
  20.4 36.8 %collective-permute-start.5 = (bf16[256,2304]{1,0:T(8,128)(2,1)}, bf16[256,2304]{1,0:T(8,128)(2,1)}, u32[]{:S(2)}, u32[]{:S(2)}) collective-permute-start(bf16[256,2304]{1,0:T(8,128)(2,1)} %copy.54.own_ref.refs_6_), channel_id=1, source_target_pairs={{0,32},{32,0},{1,33},{33,1},{2,34},{34,2},{3,35},{35,3},{4,36},{36... | collective-permute-start | bytes 3538952 | tf_op jit(solution)/shard_map/ppermute | solution.py:564
  32.3 15.5 %collective-permute-start.8 = (bf16[128,2304]{1,0:T(8,128)(2,1)S(1)}, bf16[128,2304]{1,0:T(8,128)(2,1)S(1)}, u32[]{:S(2)}, u32[]{:S(2)}) collective-permute-start(bf16[128,2304]{1,0:T(8,128)(2,1)S(1)} %collective-permute-done.6.up_ref.refs_8_), channel_id=1, source_target_pairs={{0,32},{32,0},{1,33},{33,1},{2,34},{34,2},{3,35},{35,3},{4,36},{36... | collective-permute-start | bytes 1769480 | tf_op jit(solution)/shard_map/ppermute | solution.py:567
  33.8 22.8 %collective-permute-start.9 = (bf16[128,2304]{1,0:T(8,128)(2,1)S(1)}, bf16[128,2304]{1,0:T(8,128)(2,1)S(1)}, u32[]{:S(2)}, u32[]{:S(2)}) collective-permute-start(bf16[128,2304]{1,0:T(8,128)(2,1)S(1)} %collective-permute-done.7.down_ref.refs_9_), channel_id=1, source_target_pairs={{0,32},{32,0},{1,33},{33,1},{2,34},{34,2},{3,35},{35,3},{4,36},{36... | collective-permute-start | bytes 1769480 | tf_op jit(solution)/shard_map/ppermute | solution.py:568
  56.6 23.3 %collective-permute-start.10 = (bf16[256,2048]{1,0:T(8,128)(2,1)}, bf16[256,2048]{1,0:T(8,128)(2,1)S(1)}, u32[]{:S(2)}, u32[]{:S(2)}) collective-permute-start(bf16[256,2048]{1,0:T(8,128)(2,1)} %copy-done.13), channel_id=1, source_target_pairs={{0,32},{32,0},{1,33},{33,1},{2,34},{34,2},{3,35},{35,3},{4,36},{36... | collective-permute-start | bytes 3145736 | tf_op jit(solution)/shard_map/ppermute | solution.py:564
  57.2 29.7 %collective-permute-start.15 = (bf16[512,1024]{1,0:T(8,128)(2,1)}, bf16[512,1024]{1,0:T(8,128)(2,1)S(1)}, u32[]{:S(2)}, u32[]{:S(2)}) collective-permute-start(bf16[512,1024]{1,0:T(8,128)(2,1)} %own_ref), channel_id=1, source_target_pairs={{0,32},{32,0},{1,33},{33,1},{2,34},{34,2},{3,35},{35,3},{4,36},{36... | collective-permute-start | bytes 3145736 | tf_op jit(solution)/shard_map/ppermute | solution.py:564
  58.5 21.5 %collective-permute-start.14 = (bf16[128,2048]{1,0:T(8,128)(2,1)}, bf16[128,2048]{1,0:T(8,128)(2,1)S(1)}, u32[]{:S(2)}, u32[]{:S(2)}) collective-permute-start(bf16[128,2048]{1,0:T(8,128)(2,1)} %copy-done.4), channel_id=1, source_target_pairs={{0,32},{32,0},{1,33},{33,1},{2,34},{34,2},{3,35},{35,3},{4,36},{36... | collective-permute-start | bytes 1572872 | tf_op jit(solution)/shard_map/ppermute | solution.py:568
  58.9 27.9 %collective-permute-start.18 = (bf16[256,1024]{1,0:T(8,128)(2,1)}, bf16[256,1024]{1,0:T(8,128)(2,1)S(1)}, u32[]{:S(2)}, u32[]{:S(2)}) collective-permute-start(bf16[256,1024]{1,0:T(8,128)(2,1)} %collective-permute-done.16.up_ref), channel_id=1, source_target_pairs={{0,32},{32,0},{1,33},{33,1},{2,34},{34,2},{3,35},{35,3},{4,36},{36... | collective-permute-start | bytes 1572872 | tf_op jit(solution)/shard_map/ppermute | solution.py:567
  59.6 27.2 %collective-permute-start.19 = (bf16[256,1024]{1,0:T(8,128)(2,1)}, bf16[256,1024]{1,0:T(8,128)(2,1)S(1)}, u32[]{:S(2)}, u32[]{:S(2)}) collective-permute-start(bf16[256,1024]{1,0:T(8,128)(2,1)} %collective-permute-done.17.down_ref), channel_id=1, source_target_pairs={{0,32},{32,0},{1,33},{33,1},{2,34},{34,2},{3,35},{35,3},{4,36},{36... | collective-permute-start | bytes 1572872 | tf_op jit(solution)/shard_map/ppermute | solution.py:568
  168.9 29.9 %collective-permute-start.92 = (bf16[2,512,1024]{2,1,0:T(8,128)(2,1)}, bf16[2,512,1024]{2,1,0:T(8,128)(2,1)}, u32[]{:S(2)}, u32[]{:S(2)}) collective-permute-start(bf16[2,512,1024]{2,1,0:T(8,128)(2,1)} %dynamic-slice_bitcast_fusion.1), channel_id=1, source_target_pairs={{0,32},{32,0},{1,33},{33,1},{2,34},{34,2},{3,35},{35,3},{4,36},{36... | collective-permute-start | bytes 6291464 | tf_op jit(solution)/shard_map/ppermute | solution.py:614
  186.9 19.9 %collective-permute-start.30 = (bf16[2,256,2048]{2,1,0:T(8,128)(2,1)}, bf16[2,256,2048]{2,1,0:T(8,128)(2,1)}, u32[]{:S(2)}, u32[]{:S(2)}) collective-permute-start(bf16[2,256,2048]{2,1,0:T(8,128)(2,1)} %dynamic-slice_bitcast_fusion.2), channel_id=1, source_target_pairs={{0,32},{32,0},{1,33},{33,1},{2,34},{34,2},{3,35},{35,3},{4,36},{36... | collective-permute-start | bytes 6291464 | tf_op jit(solution)/shard_map/ppermute | solution.py:614
  202.4 16.6 %collective-permute-start.94 = (bf16[2,128,512]{2,1,0:T(8,128)(2,1)S(1)}, bf16[2,128,512]{2,1,0:T(8,128)(2,1)S(1)}, u32[]{:S(2)}, u32[]{:S(2)}) collective-permute-start(bf16[2,128,512]{2,1,0:T(8,128)(2,1)S(1)} %get-tuple-element.84), channel_id=1, source_target_pairs={{0,4},{2,6},{4,0},{6,2},{1,5},{3,7},{5,1},{7,3},{8,12},{10,14},{12... | collective-permute-start | bytes 786440 | tf_op jit(solution)/shard_map/ppermute | solution.py:585
  219.0 18.0 %collective-permute-start.32 = (bf16[2,64,1024]{2,1,0:T(8,128)(2,1)S(1)}, bf16[2,64,1024]{2,1,0:T(8,128)(2,1)S(1)}, u32[]{:S(2)}, u32[]{:S(2)}) collective-permute-start(bf16[2,64,1024]{2,1,0:T(8,128)(2,1)S(1)} %get-tuple-element.90), channel_id=1, source_target_pairs={{0,4},{2,6},{4,0},{6,2},{1,5},{3,7},{5,1},{7,3},{8,12},{10,14},{12... | collective-permute-start | bytes 786440 | tf_op jit(solution)/shard_map/ppermute | solution.py:585
  219.8 17.2 %collective-permute-start.33 = (bf16[2,64,1024]{2,1,0:T(8,128)(2,1)S(1)}, bf16[2,64,1024]{2,1,0:T(8,128)(2,1)S(1)}, u32[]{:S(2)}, u32[]{:S(2)}) collective-permute-start(bf16[2,64,1024]{2,1,0:T(8,128)(2,1)S(1)} %get-tuple-element.89), channel_id=1, source_target_pairs={{0,6},{2,0},{4,2},{6,4},{1,7},{3,1},{5,3},{7,5},{8,14},{10,8},{12,... | collective-permute-start | bytes 786440 | tf_op jit(solution)/shard_map/ppermute | solution.py:585
  223.3 15.5 %collective-permute-start.46 = (bf16[2,64,1024]{2,1,0:T(8,128)(2,1)S(1)}, bf16[2,64,1024]{2,1,0:T(8,128)(2,1)S(1)}, u32[]{:S(2)}, u32[]{:S(2)}) collective-permute-start(bf16[2,64,1024]{2,1,0:T(8,128)(2,1)S(1)} %get-tuple-element.91), channel_id=1, source_target_pairs={{0,8},{8,16},{16,24},{24,0},{1,9},{9,17},{17,25},{25,1},{2,10},{10... | collective-permute-start | bytes 786440 | tf_op jit(solution)/shard_map/ppermute | solution.py:585
  258.3 16.9 %collective-permute-start.115 = (bf16[32,512]{1,0:T(8,128)(2,1)S(1)}, bf16[32,512]{1,0:T(8,128)(2,1)S(1)}, u32[]{:S(2)}, u32[]{:S(2)}) collective-permute-start(bf16[32,512]{1,0:T(8,128)(2,1)S(1)} %get-tuple-element.128), channel_id=1, source_target_pairs={{0,65},{64,0},{1,64},{65,1},{2,67},{66,2},{3,66},{67,3},{4,69},{68... | collective-permute-start | bytes 98312 | tf_op jit(solution)/shard_map/ppermute | solution.py:604
  261.0 14.9 %collective-permute-start.116 = (bf16[32,512]{1,0:T(8,128)(2,1)S(1)}, bf16[32,512]{1,0:T(8,128)(2,1)S(1)}, u32[]{:S(2)}, u32[]{:S(2)}) collective-permute-start(bf16[32,512]{1,0:T(8,128)(2,1)S(1)} %get-tuple-element.128), channel_id=1, source_target_pairs={{0,64},{64,1},{1,65},{65,0},{2,66},{66,3},{3,67},{67,2},{4,68},{68... | collective-permute-start | bytes 98312 | tf_op jit(solution)/shard_map/ppermute | solution.py:603
  266.4 19.5 %collective-permute-start.38 = (bf16[16,1024]{1,0:T(8,128)(2,1)S(1)}, bf16[16,1024]{1,0:T(8,128)(2,1)S(1)}, u32[]{:S(2)}, u32[]{:S(2)}) collective-permute-start(bf16[16,1024]{1,0:T(8,128)(2,1)S(1)} %get-tuple-element.130), channel_id=1, source_target_pairs={{0,65},{64,0},{1,64},{65,1},{2,67},{66,2},{3,66},{67,3},{4,69},{68... | collective-permute-start | bytes 98312 | tf_op jit(solution)/shard_map/ppermute | solution.py:604
  266.5 20.2 %collective-permute-start.39 = (bf16[16,1024]{1,0:T(8,128)(2,1)S(1)}, bf16[16,1024]{1,0:T(8,128)(2,1)S(1)}, u32[]{:S(2)}, u32[]{:S(2)}) collective-permute-start(bf16[16,1024]{1,0:T(8,128)(2,1)S(1)} %get-tuple-element.130), channel_id=1, source_target_pairs={{0,64},{64,1},{1,65},{65,0},{2,66},{66,3},{3,67},{67,2},{4,68},{68... | collective-permute-start | bytes 98312 | tf_op jit(solution)/shard_map/ppermute | solution.py:603
  273.9 16.1 %collective-permute-start.53 = (bf16[16,1024]{1,0:T(8,128)(2,1)S(1)}, bf16[16,1024]{1,0:T(8,128)(2,1)S(1)}, u32[]{:S(2)}, u32[]{:S(2)}) collective-permute-start(bf16[16,1024]{1,0:T(8,128)(2,1)S(1)} %get-tuple-element.132), channel_id=1, source_target_pairs={{0,65},{64,0},{1,64},{65,1},{2,67},{66,2},{3,66},{67,3},{4,69},{68... | collective-permute-start | bytes 98312 | tf_op jit(solution)/shard_map/ppermute | solution.py:604
  275.2 15.2 %collective-permute-start.54 = (bf16[16,1024]{1,0:T(8,128)(2,1)S(1)}, bf16[16,1024]{1,0:T(8,128)(2,1)S(1)}, u32[]{:S(2)}, u32[]{:S(2)}) collective-permute-start(bf16[16,1024]{1,0:T(8,128)(2,1)S(1)} %get-tuple-element.132), channel_id=1, source_target_pairs={{0,64},{64,1},{1,65},{65,0},{2,66},{66,3},{3,67},{67,2},{4,68},{68... | collective-permute-start | bytes 98312 | tf_op jit(solution)/shard_map/ppermute | solution.py:603
  310.6 34.6 %collective-permute-start.62 = (bf16[2,64,1152]{2,1,0:T(8,128)(2,1)S(1)}, bf16[2,64,1152]{2,1,0:T(8,128)(2,1)S(1)}, u32[]{:S(2)}, u32[]{:S(2)}) collective-permute-start(bf16[2,64,1152]{2,1,0:T(8,128)(2,1)S(1)} %get-tuple-element.76), channel_id=1, source_target_pairs={{0,2},{2,4},{4,6},{6,0},{1,3},{3,5},{5,7},{7,1},{8,10},{10,12},{12... | collective-permute-start | bytes 884744 | tf_op jit(solution)/shard_map/ppermute | solution.py:585
  311.6 33.7 %collective-permute-start.63 = (bf16[2,64,1152]{2,1,0:T(8,128)(2,1)S(1)}, bf16[2,64,1152]{2,1,0:T(8,128)(2,1)S(1)}, u32[]{:S(2)}, u32[]{:S(2)}) collective-permute-start(bf16[2,64,1152]{2,1,0:T(8,128)(2,1)S(1)} %get-tuple-element.78), channel_id=1, source_target_pairs={{0,4},{2,6},{4,0},{6,2},{1,5},{3,7},{5,1},{7,3},{8,12},{10,14},{12... | collective-permute-start | bytes 884744 | tf_op jit(solution)/shard_map/ppermute | solution.py:585
  (128 other events, 1114.4 us)
